TPU v7x, 256 devices: a whole 4x4x8 slice. The times are simulated.
256 devices in a mesh: dom: 64 (over y, z, core), kv: 4 (over x).
Axes of the slice: x: 4, y: 4, z: 8, core: 2. Of those that a mesh axis runs over, the one named last changes fastest.
Arguments:
- node_feats: bfloat16 [32768, 128], P(('dom', 'kv')), may hold values from -11 to 11
- positions: float32 [3, 32768], P(None, ('dom', 'kv')), may hold values from 0 to 2304, as said below
- species: int32 [32768], P(('dom', 'kv')), may hold values from 0 to 1
- halo_rows: int32 [256, 64], P(('dom', 'kv')), may hold values from 0 to 127, as said below
- neighbours: int32 [32768, 32], P(('dom', 'kv')), may hold values from 0 to 191, as said below
- nbr_count: int32 [32768], P(('dom', 'kv')), may hold values from 16 to 32, as said below
- recip_vectors: int32 [3, 16384], replicated, may hold values from -13 to 13, as said below
- w_msg: bfloat16 [128, 128], replicated, may hold values from -0.5 to 0.5
- w_rad1: bfloat16 [8, 128], replicated, may hold values from -2 to 2
- w_rad2: bfloat16 [128, 256], replicated, may hold values from -0.5 to 0.5
- w_upd: bfloat16 [384, 128], replicated, may hold values from -0.3125 to 0.3125
- w_out: bfloat16 [128], replicated, may hold values from -0.5 to 0.5
- chi_table: float32 [2], replicated, may hold values from -1 to 1
- hard_table: float32 [2], replicated, may hold values from 0.5 to 2
Outputs:
- electroneg: float32 [32768], P(('dom', 'kv'))
- charges: float32 [32768], P(('dom', 'kv'))
Inputs may be any that keep to these rules, and one draw needn't show every extreme that they name: `halo_rows`: in each slab's row, 64 distinct local atom indices; the first 32 lie near the slab's lower face, the rest near its upper face. `neighbours`: an atom never lists its own local index. `nbr_count`: the first atom of every slab has all 32 slots live. `recip_vectors`: distinct nonzero triples. `positions`: atoms of slab s have first coordinate in [9 s, 9 (s + 1)), the other two in [0, 20).
All inputs are finite; a program needn't handle non-finite values.
Results may differ from a plain program's by a relative error of at most 0.003.
Values may be sent and summed in bfloat16 or wider, within the bound.
A program may use at most 128 MiB of HBM per device.

v0:
```python
import math
import jax
import jax.numpy as jnp
from jax import lax
from jax.sharding import PartitionSpec as P

ITERS = 4
slab_width = 9.0
side_length = 20.0
two_pi = 2.0 * math.pi
highest = lax.Precision.HIGHEST


def with_halo(block, sides, width):
    for axis, dim in sides:
        count = lax.axis_size(axis)
        forward = [(i, i + 1) for i in range(count - 1)]
        forward.append((count - 1, 0))
        backward = [(target, source) for source, target in forward]
        low = lax.ppermute(
            lax.slice_in_dim(block, block.shape[dim] - width, None, axis=dim), axis, forward
        )
        high = lax.ppermute(lax.slice_in_dim(block, 0, width, axis=dim), axis, backward)
        block = jnp.concatenate([low, block, high], axis=dim)
    return block


def wrapped(offset, length):
    return jnp.where(
        offset > 0.5 * length,
        offset - length,
        jnp.where(offset < -0.5 * length, offset + length, offset),
    )


def recip_setup(coords, triples, box_x, atoms_total):
    comp_x = triples[0].astype(jnp.float32)
    comp_y = triples[1].astype(jnp.float32)
    comp_z = triples[2].astype(jnp.float32)
    phase_arg = two_pi * (
        coords[0][:, None] * (comp_x / box_x)[None, :]
        + coords[1][:, None] * (comp_y / side_length)[None, :]
        + coords[2][:, None] * (comp_z / side_length)[None, :]
    )
    phase_table = jnp.concatenate([jnp.cos(phase_arg), jnp.sin(phase_arg)], axis=1)
    m_square = comp_x * comp_x + comp_y * comp_y + comp_z * comp_z
    weight = 16.0 / atoms_total * jnp.exp(-m_square / 400.0) / (1.0 + m_square / 16.0)
    return (phase_table, weight)


def message_layer(
    ext_proj,
    ext_pos,
    own_pos,
    own_feats,
    nbr_index,
    counts,
    kinds,
    w_rad1,
    w_rad2,
    w_upd,
    w_out,
    chi_table,
    box_x,
):
    atoms_dev, slot_count = nbr_index.shape
    channels = own_feats.shape[1]
    flat_index = nbr_index.reshape(-1)
    nbr_proj = jnp.take(ext_proj, flat_index, axis=0).reshape(atoms_dev, slot_count, channels)
    nbr_pos = jnp.take(ext_pos, flat_index, axis=1).reshape(3, atoms_dev, slot_count)
    displace = jnp.stack(
        [
            wrapped(nbr_pos[0] - own_pos[0][:, None], box_x),
            wrapped(nbr_pos[1] - own_pos[1][:, None], side_length),
            wrapped(nbr_pos[2] - own_pos[2][:, None], side_length),
        ]
    )
    distance = jnp.sqrt(jnp.sum(displace * displace, axis=0) + 0.25)
    unit_vec = displace / distance
    basis_count = w_rad1.shape[0]
    centres = 1.0 + 1.25 * jnp.arange(basis_count, dtype=jnp.float32)
    radial_basis = jnp.exp(-jnp.square((distance[:, :, None] - centres) / 1.25)).astype(
        jnp.bfloat16
    )
    hidden = jax.nn.silu(
        jnp.dot(radial_basis.reshape(-1, basis_count), w_rad1, preferred_element_type=jnp.float32)
    ).astype(jnp.bfloat16)
    radial = jnp.dot(hidden, w_rad2, preferred_element_type=jnp.float32).reshape(
        atoms_dev, slot_count, 2 * channels
    )
    live_mask = (jnp.arange(slot_count)[None, :] < counts[:, None]).astype(jnp.float32)
    radial = radial * live_mask[:, :, None]
    msg_scale = 1.0 / math.sqrt(slot_count)
    scalar_msg = jnp.sum(radial[:, :, :channels] * nbr_proj, axis=1) * msg_scale
    carried = radial[:, :, channels:] * nbr_proj
    vector_msg = jnp.sum(unit_vec[:, :, :, None] * carried[None], axis=2) * msg_scale
    vec_square = jnp.sum(vector_msg * vector_msg, axis=0)
    joined = jnp.concatenate(
        [scalar_msg, vec_square, own_feats.astype(jnp.float32)], axis=1
    ).astype(jnp.bfloat16)
    update = jax.nn.silu(jnp.dot(joined, w_upd, preferred_element_type=jnp.float32)).astype(
        jnp.bfloat16
    )
    one_hot = (kinds[:, None] == jnp.arange(chi_table.shape[0])[None, :]).astype(jnp.float32)
    return jnp.dot(update, w_out, preferred_element_type=jnp.float32) + jnp.sum(
        one_hot * chi_table[None, :], axis=1
    )


def squares(residual):
    return lax.psum(jnp.sum(residual * residual, axis=1), ("dom", "kv"))


def local(
    node_feats,
    positions,
    species,
    halo_rows,
    neighbours,
    nbr_count,
    recip_vectors,
    w_msg,
    w_rad1,
    w_rad2,
    w_upd,
    w_out,
    chi_table,
    hard_table,
):
    atoms_dev = node_feats.shape[0]
    halo_width = halo_rows.shape[1] // 2
    slab_count = lax.axis_size("dom") * lax.axis_size("kv")
    box_x = slab_count * slab_width
    atoms_total = atoms_dev * slab_count
    send_rows = halo_rows[0]
    packet_feats = jnp.take(node_feats, send_rows, axis=0)
    packet_pos = jnp.take(positions, send_rows, axis=1).T
    got_feats = with_halo(packet_feats, ((("dom", "kv"), 0),), halo_width)
    got_pos = with_halo(packet_pos, ((("dom", "kv"), 0),), halo_width)
    own_proj = jnp.dot(node_feats, w_msg, preferred_element_type=jnp.float32).astype(jnp.bfloat16)
    far_feats = jnp.concatenate([got_feats[:halo_width], got_feats[3 * halo_width :]], axis=0)
    far_proj = jnp.dot(far_feats, w_msg, preferred_element_type=jnp.float32).astype(jnp.bfloat16)
    ext_proj = jnp.concatenate([own_proj, far_proj], axis=0)
    ext_pos = jnp.concatenate(
        [positions, got_pos[:halo_width].T, got_pos[3 * halo_width :].T], axis=1
    )
    electroneg = message_layer(
        ext_proj,
        ext_pos,
        positions,
        node_feats,
        neighbours,
        nbr_count,
        species,
        w_rad1,
        w_rad2,
        w_upd,
        w_out,
        chi_table,
        box_x,
    )
    one_hot = (species[:, None] == jnp.arange(hard_table.shape[0])[None, :]).astype(jnp.float32)
    hardness = jnp.sum(one_hot * hard_table[None, :], axis=1)
    phase_table, weight = recip_setup(positions, recip_vectors, box_x, atoms_total)
    weight_pair = jnp.concatenate([weight, weight])
    right_side = jnp.stack([-electroneg, jnp.ones_like(electroneg)])
    solution = jnp.zeros_like(right_side)
    residual = right_side
    direction = right_side
    norm_now = squares(residual)
    for iteration in range(ITERS):
        partial_value = jnp.dot(
            direction, phase_table, precision=highest, preferred_element_type=jnp.float32
        )
        summed = lax.psum(partial_value, ("dom", "kv"))
        potential = lax.dot_general(
            summed * weight_pair,
            phase_table,
            (((1,), (1,)), ((), ())),
            precision=highest,
            preferred_element_type=jnp.float32,
        )
        applied = hardness * direction + potential
        curvature = lax.psum(jnp.sum(direction * applied, axis=1), ("dom", "kv"))
        step_size = norm_now / curvature
        solution = solution + step_size[:, None] * direction
        residual = residual - step_size[:, None] * applied
        if iteration + 1 < ITERS:
            norm_next = squares(residual)
            direction = residual + (norm_next / norm_now)[:, None] * direction
            norm_now = norm_next
    totals = lax.psum(jnp.sum(solution, axis=1), ("dom", "kv"))
    charges = solution[0] - totals[0] / totals[1] * solution[1]
    return (electroneg, charges)


def solution(mesh):
    return jax.shard_map(
        local,
        mesh=mesh,
        in_specs=(
            P(("dom", "kv"), None),
            P(None, ("dom", "kv")),
            P(("dom", "kv")),
            P(("dom", "kv"), None),
            P(("dom", "kv"), None),
            P(("dom", "kv")),
            P(),
            P(),
            P(),
            P(),
            P(),
            P(),
            P(),
            P(),
        ),
        out_specs=(P(("dom", "kv")), P(("dom", "kv"))),
        check_vma=False,
    )
```

profile of v0, /device:TPU:1, one launch (start us, length us, event | category | flops | bytes accessed | tf_op | source)
XLA Modules:
  0.0 1828.8 jit_solution(18002408356740054125)
XLA Ops:
  7.2 0.7 compare_and_fusion.2
  7.9 0.7 fusion.49
  8.6 1.4 gather_fusion.2
  10.0 2.1 collective-permute-start.2
  12.1 1.9 collective-permute-start.3
  14.1 0.8 copy.50
  14.8 0.6 gather_fusion
  15.6 3.1 collective-permute-start.1
  18.8 0.8 slice_bitcast_fusion.2
  19.6 0.7 compare_and_fusion
  20.3 0.8 copy.48
  21.3 0.9 convolution_convert_fusion
  22.2 0.7 fusion.35
  23.0 1.6 multiply_divide_fusion
  24.6 0.8 select_reduce_fusion
  25.4 33.0 %fusion.1 = (f32[128,16384]{1,0:T(8,128)}, f32[128,16384]{1,0:T(8,128)}) fusion(f32[16384]{0:T(1024)S(1)} %bitcast.46, f32[128]{0:T(128)S(1)} %get-tuple-element.32, f32[16384]{0:T(1024)S(1)} %bitcast.47, f32[128]{0:T(128)S(1)} %get-tuple-element.33, f32[16384]{0:T(1024)S(1)} %bitcast.45, f32[128]{0:T(128)S(1)} %get-tuple-element.31), kind=kLoop, calls=%fused_computation.7 | loop fusion | flops 12582912 | bytes 16975360 | tf_op jit(solution)/shard_map/cos | solution.py:45
  58.5 10.8 gather_fusion.1
  69.3 2.1 select_bitcast_fusion
  71.5 2.8 slice_reduce_fusion.2
  75.2 3.3 fusion.3
  78.5 3.9 broadcast_multiply_fusion
  82.7 12.1 gather_fusion.3
  94.9 3.3 fusion.2
  98.2 2.2 multiply_reduce_fusion
  100.5 0.3 fusion.6
  100.8 13.9 fusion.41
  114.8 253.6 %all-reduce.7.cloned.1.call-done = f32[2,32768]{1,0:T(2,128)} async-done(((f32[2,32768]{1,0:T(2,128)}), f32[2,32768]{1,0:T(2,128)}) %all-reduce.7.cloned.1.call-update) | async-done | bytes 262160 | tf_op jit(solution)/shard_map/psum | solution.py:175
  368.4 16.8 fusion.44
  385.2 77.9 %all-reduce.1 = (f32[2]{0:T(128)S(1)}, f32[2]{0:T(128)S(1)}) all-reduce(f32[2]{0:T(128)S(1)} %get-tuple-element.6, f32[2]{0:T(128)S(1)} %get-tuple-element.5), channel_id=1, replica_groups=mesh['dom'=64,'kv'=4] {'dom','kv'}, use_global_device_ids=true, to_apply=%region_6.7 | all-reduce | flops 4 | bytes 32 | tf_op jit(solution)/shard_map/psum | solution.py:111
  463.2 73.2 %psum.94 = f32[2]{0:T(128)S(1)} all-reduce(f32[2]{0:T(128)S(1)} %get-tuple-element.17), channel_id=1, replica_groups=mesh['dom'=64,'kv'=4] {'dom','kv'}, use_global_device_ids=true, to_apply=%region_12.13 | all-reduce | flops 2 | bytes 16 | tf_op jit(solution)/shard_map/psum | solution.py:111
  536.5 13.6 fusion.61
  550.2 245.8 %all-reduce.9.cloned.1.call-done = f32[2,32768]{1,0:T(2,128)} async-done(((f32[2,32768]{1,0:T(2,128)}), f32[2,32768]{1,0:T(2,128)}) %all-reduce.9.cloned.1.call-update) | async-done | bytes 262160 | tf_op jit(solution)/shard_map/psum | solution.py:175
  796.0 16.9 multiply_reduce_fusion.6
  812.9 77.4 %psum.96 = f32[2]{0:T(128)S(1)} all-reduce(f32[2]{0:T(128)S(1)} %get-tuple-element.37), channel_id=1, replica_groups=mesh['dom'=64,'kv'=4] {'dom','kv'}, use_global_device_ids=true, to_apply=%region_15.16 | all-reduce | flops 2 | bytes 16 | tf_op jit(solution)/shard_map/psum | solution.py:184
  890.5 73.4 %psum.97 = f32[2]{0:T(128)S(1)} all-reduce(f32[2]{0:T(128)S(1)} %get-tuple-element.15), channel_id=1, replica_groups=mesh['dom'=64,'kv'=4] {'dom','kv'}, use_global_device_ids=true, to_apply=%region_17.18 | all-reduce | flops 2 | bytes 16 | tf_op jit(solution)/shard_map/psum | solution.py:111
  964.1 13.6 fusion.60
  977.7 245.9 %all-reduce.11.cloned.1.call-done = f32[2,32768]{1,0:T(2,128)} async-done(((f32[2,32768]{1,0:T(2,128)}), f32[2,32768]{1,0:T(2,128)}) %all-reduce.11.cloned.1.call-update) | async-done | bytes 262160 | tf_op jit(solution)/shard_map/psum | solution.py:175
  1223.7 17.0 multiply_reduce_fusion.4
  1240.7 77.4 %psum.99 = f32[2]{0:T(128)S(1)} all-reduce(f32[2]{0:T(128)S(1)} %get-tuple-element.39), channel_id=1, replica_groups=mesh['dom'=64,'kv'=4] {'dom','kv'}, use_global_device_ids=true, to_apply=%region_20.21 | all-reduce | flops 2 | bytes 16 | tf_op jit(solution)/shard_map/psum | solution.py:184
  1318.3 73.5 %psum.100 = f32[2]{0:T(128)S(1)} all-reduce(f32[2]{0:T(128)S(1)} %get-tuple-element.13), channel_id=1, replica_groups=mesh['dom'=64,'kv'=4] {'dom','kv'}, use_global_device_ids=true, to_apply=%region_22.23 | all-reduce | flops 2 | bytes 16 | tf_op jit(solution)/shard_map/psum | solution.py:111
  1391.8 13.6 fusion.59
  1405.4 245.9 %all-reduce.13.cloned.1.call-done = f32[2,32768]{1,0:T(2,128)} async-done(((f32[2,32768]{1,0:T(2,128)}), f32[2,32768]{1,0:T(2,128)}) %all-reduce.13.cloned.1.call-update) | async-done | bytes 262160 | tf_op jit(solution)/shard_map/psum | solution.py:175
  1651.3 17.1 fusion.5
  1668.4 77.4 %psum.102 = f32[2]{0:T(128)S(1)} all-reduce(f32[2]{0:T(128)S(1)} %fusion.5), channel_id=1, replica_groups=mesh['dom'=64,'kv'=4] {'dom','kv'}, use_global_device_ids=true, to_apply=%region_25.26 | all-reduce | flops 2 | bytes 16 | tf_op jit(solution)/shard_map/psum | solution.py:184
  1745.8 0.2 fusion.62
  1746.0 73.2 %psum.103 = f32[2]{0:T(128)S(1)} all-reduce(f32[2]{0:T(128)S(1)} %get-tuple-element.11), channel_id=1, replica_groups=mesh['dom'=64,'kv'=4] {'dom','kv'}, use_global_device_ids=true, to_apply=%region_27.28 | all-reduce | flops 2 | bytes 16 | tf_op jit(solution)/shard_map/psum | solution.py:192
  1819.3 0.6 fusion.66
  1821.2 0.5 subtract_bitcast_fusion
  (71 shorter events, 2.7 us)
Async XLA Ops:
  7.2 93.3 %copy-start = (bf16[384,128]{1,0:T(8,128)(2,1)S(1)}, bf16[384,128]{1,0:T(8,128)(2,1)}, u32[]{:S(2)}) copy-start(bf16[384,128]{1,0:T(8,128)(2,1)} %param.24) | copy-start | bytes 294916
  7.2 361.2 %all-reduce.7.cloned.1.call-start = ((), (), s32[]{:S(2)}) async-start(), calls=%async_computation | async-start | bytes 524288 | tf_op jit(solution)/shard_map/psum | solution.py:175
  10.0 72.5 %collective-permute-start.2 = (bf16[32,128]{1,0:T(8,128)(2,1)S(1)}, bf16[32,128]{1,0:T(8,128)(2,1)S(1)}, u32[]{:S(2)}, u32[]{:S(2)}) collective-permute-start(bf16[32,128]{1,0:T(8,128)(2,1)S(1)} %get-tuple-element.29), channel_id=1, source_target_pairs={{0,1},{1,2},{2,3},{3,4},{4,5},{5,6},{6,7},{7,8},{8,9},{9,10},{10,1... | collective-permute-start | bytes 24584 | tf_op jit(solution)/shard_map/ppermute | solution.py:20
  12.1 70.4 %collective-permute-start.3 = (bf16[32,128]{1,0:T(8,128)(2,1)S(1)}, bf16[32,128]{1,0:T(8,128)(2,1)S(1)}, u32[]{:S(2)}, u32[]{:S(2)}) collective-permute-start(bf16[32,128]{1,0:T(8,128)(2,1)S(1)} %get-tuple-element.30), channel_id=1, source_target_pairs={{1,0},{2,1},{3,2},{4,3},{5,4},{6,5},{7,6},{8,7},{9,8},{10,9},{11,1... | collective-permute-start | bytes 24584 | tf_op jit(solution)/shard_map/ppermute | solution.py:23
  15.5 43.0 %collective-permute-start = (f32[32,3]{1,0:T(8,128)S(1)}, f32[32,3]{1,0:T(8,128)S(1)}, u32[]{:S(2)}, u32[]{:S(2)}) collective-permute-start(f32[32,3]{1,0:T(8,128)S(1)} %get-tuple-element.27), channel_id=1, source_target_pairs={{0,1},{1,2},{2,3},{3,4},{4,5},{5,6},{6,7},{7,8},{8,9},{9,10},{10,1... | collective-permute-start | bytes 1160 | tf_op jit(solution)/shard_map/ppermute | solution.py:20
  15.6 42.9 %collective-permute-start.1 = (f32[32,3]{1,0:T(8,128)S(1)}, f32[32,3]{1,0:T(8,128)S(1)}, u32[]{:S(2)}, u32[]{:S(2)}) collective-permute-start(f32[32,3]{1,0:T(8,128)S(1)} %get-tuple-element.28), channel_id=1, source_target_pairs={{1,0},{2,1},{3,2},{4,3},{5,4},{6,5},{7,6},{8,7},{9,8},{10,9},{11,1... | collective-permute-start | bytes 1160 | tf_op jit(solution)/shard_map/ppermute | solution.py:23
  58.4 16.8 copy-start.3
  58.4 16.8 copy-start.4
  75.2 7.4 copy-start.2
  82.7 17.8 copy-start.1
  82.7 17.8 copy-start.5
  100.8 13.9 copy-start.6
  114.7 681.3 %all-reduce.9.cloned.1.call-start = ((), (), s32[]{:S(2)}) async-start(), calls=%async_computation.1 | async-start | bytes 524288 | tf_op jit(solution)/shard_map/psum | solution.py:175
  550.1 673.5 %all-reduce.11.cloned.1.call-start = ((), (), s32[]{:S(2)}) async-start(), calls=%async_computation.2 | async-start | bytes 524288 | tf_op jit(solution)/shard_map/psum | solution.py:175
  977.7 673.6 %all-reduce.13.cloned.1.call-start = ((), (), s32[]{:S(2)}) async-start(), calls=%async_computation.3 | async-start | bytes 524288 | tf_op jit(solution)/shard_map/psum | solution.py:175
Sparse Core Ops, SparseCore 0:
  114.9 253.4 all-reduce.6
  550.2 245.7 all-reduce.8
  977.8 245.8 all-reduce.10
  1405.6 245.7 all-reduce.12
where the time goes:
time: 1830 us
  waiting for transfers between devices  991 us (54%)
  blocking collectives  604 us (33%)
  matrix products  127 us (7%)
  other arithmetic  51.7 us (3%)
  local copies, waits for them, and re-layouts  31.7 us (2%)
    psum x4, waiting for transfers between devices, local(): summed = lax.psum(partial_value, ('dom', 'kv'))  991 us
    psum x4, blocking collectives, squares(): return lax.psum(jnp.sum(residual * residual, axis=1), ('dom', 'kv'))  298 us
    psum x3, blocking collectives, local(): curvature = lax.psum(jnp.sum(direction * applied, axis=1), ('dom', 'kv'))  232 us
    psum x1, blocking collectives, local(): totals = lax.psum(jnp.sum(solution, axis=1), ('dom', 'kv'))  73.2 us
    dot_general x4, matrix products, local(): lax.dot_general(summed * weight_pair, phase_table, (((1,), (1,)), ((), ()...  67.8 us
    dot_general x4, matrix products, local(): jnp.dot(direction, phase_table, precision=highest, preferred_element_type...  54.7 us
  transfers between devices with their start and end apart: 8, of which 4 were waited for; matrix products, arithmetic and copies ran while one was open for 4% of the time, Pallas kernels for 0%

commit v1 on v0

--- a/solution.py
+++ b/solution.py
@@ -189,7 +189,7 @@
             norm_next = squares(residual)
             direction = residual + (norm_next / norm_now)[:, None] * direction
             norm_now = norm_next
-    totals = lax.psum(jnp.sum(solution, axis=1), ("dom", "kv"))
+    totals = lax.psum(lax.psum(jnp.sum(solution, axis=1), "kv"), "dom")
     charges = solution[0] - totals[0] / totals[1] * solution[1]
     return (electroneg, charges)
 

time: 1830 us -> 1890 us (1.033)
  blocking collectives: 604 us -> 664 us
    psum x1 -> x2, blocking collectives: 73.2 us -> 134 us  [local(): totals = lax.psum(lax.psum(jnp.sum(solution, axis=1), 'kv'), 'dom')]
  transfers between devices with their start and end apart: 8 -> 8, of which waited for: 4 -> 4; matrix products, arithmetic and copies ran while one was open for 4% -> 3% of each run, Pallas kernels for 0% -> 0%
where the time goes in v1:
time: 1890 us
  waiting for transfers between devices  991 us (52%)
  blocking collectives  664 us (35%)
  matrix products  127 us (7%)
  other arithmetic  51.7 us (3%)
  local copies, waits for them, and re-layouts  31.7 us (2%)
    psum x4, waiting for transfers between devices, local(): summed = lax.psum(partial_value, ('dom', 'kv'))  991 us
    psum x4, blocking collectives, squares(): return lax.psum(jnp.sum(residual * residual, axis=1), ('dom', 'kv'))  298 us
    psum x3, blocking collectives, local(): curvature = lax.psum(jnp.sum(direction * applied, axis=1), ('dom', 'kv'))  232 us
    psum x2, blocking collectives, local(): totals = lax.psum(lax.psum(jnp.sum(solution, axis=1), 'kv'), 'dom')  134 us
    dot_general x4, matrix products, local(): lax.dot_general(summed * weight_pair, phase_table, (((1,), (1,)), ((), ()...  67.8 us
    dot_general x4, matrix products, local(): jnp.dot(direction, phase_table, precision=highest, preferred_element_type...  54.7 us
  transfers between devices with their start and end apart: 8, of which 4 were waited for; matrix products, arithmetic and copies ran while one was open for 3% of the time, Pallas kernels for 0%

profile of v1, /device:TPU:1, one launch (start us, length us, event | category | flops | bytes accessed | tf_op | source)
XLA Modules:
  0.0 1889.5 jit_solution(17841677040572685294)
XLA Ops:
  7.2 0.7 compare_and_fusion.2
  7.9 0.7 fusion.49
  8.6 1.4 gather_fusion.2
  10.0 2.1 collective-permute-start.2
  12.1 1.9 collective-permute-start.3
  14.1 0.8 copy.50
  14.8 0.6 gather_fusion
  15.6 3.1 collective-permute-start.1
  18.8 0.8 slice_bitcast_fusion.2
  19.6 0.7 compare_and_fusion
  20.3 0.8 copy.48
  21.3 0.9 convolution_convert_fusion
  22.2 0.7 fusion.35
  23.0 1.6 multiply_divide_fusion
  24.6 0.8 select_reduce_fusion
  25.4 33.0 %fusion.1 = (f32[128,16384]{1,0:T(8,128)}, f32[128,16384]{1,0:T(8,128)}) fusion(f32[16384]{0:T(1024)S(1)} %bitcast.46, f32[128]{0:T(128)S(1)} %get-tuple-element.32, f32[16384]{0:T(1024)S(1)} %bitcast.47, f32[128]{0:T(128)S(1)} %get-tuple-element.33, f32[16384]{0:T(1024)S(1)} %bitcast.45, f32[128]{0:T(128)S(1)} %get-tuple-element.31), kind=kLoop, calls=%fused_computation.7 | loop fusion | flops 12582912 | bytes 16975360 | tf_op jit(solution)/shard_map/cos | solution.py:45
  58.5 10.8 gather_fusion.1
  69.3 2.1 select_bitcast_fusion
  71.5 2.8 slice_reduce_fusion.2
  75.2 3.3 fusion.3
  78.5 3.9 broadcast_multiply_fusion
  82.7 12.1 gather_fusion.3
  94.9 3.3 fusion.2
  98.2 2.2 multiply_reduce_fusion
  100.5 0.3 fusion.6
  100.8 13.9 fusion.41
  114.8 253.6 %all-reduce.7.cloned.1.call-done = f32[2,32768]{1,0:T(2,128)} async-done(((f32[2,32768]{1,0:T(2,128)}), f32[2,32768]{1,0:T(2,128)}) %all-reduce.7.cloned.1.call-update) | async-done | bytes 262160 | tf_op jit(solution)/shard_map/psum | solution.py:175
  368.4 16.8 fusion.44
  385.2 77.9 %all-reduce.1 = (f32[2]{0:T(128)S(1)}, f32[2]{0:T(128)S(1)}) all-reduce(f32[2]{0:T(128)S(1)} %get-tuple-element.6, f32[2]{0:T(128)S(1)} %get-tuple-element.5), channel_id=1, replica_groups=mesh['dom'=64,'kv'=4] {'dom','kv'}, use_global_device_ids=true, to_apply=%region_6.7 | all-reduce | flops 4 | bytes 32 | tf_op jit(solution)/shard_map/psum | solution.py:111
  463.2 73.2 %psum.101 = f32[2]{0:T(128)S(1)} all-reduce(f32[2]{0:T(128)S(1)} %get-tuple-element.17), channel_id=1, replica_groups=mesh['dom'=64,'kv'=4] {'dom','kv'}, use_global_device_ids=true, to_apply=%region_12.13 | all-reduce | flops 2 | bytes 16 | tf_op jit(solution)/shard_map/psum | solution.py:111
  536.5 13.6 fusion.61
  550.2 245.8 %all-reduce.9.cloned.1.call-done = f32[2,32768]{1,0:T(2,128)} async-done(((f32[2,32768]{1,0:T(2,128)}), f32[2,32768]{1,0:T(2,128)}) %all-reduce.9.cloned.1.call-update) | async-done | bytes 262160 | tf_op jit(solution)/shard_map/psum | solution.py:175
  796.0 16.9 multiply_reduce_fusion.6
  812.9 77.4 %psum.103 = f32[2]{0:T(128)S(1)} all-reduce(f32[2]{0:T(128)S(1)} %get-tuple-element.37), channel_id=1, replica_groups=mesh['dom'=64,'kv'=4] {'dom','kv'}, use_global_device_ids=true, to_apply=%region_15.16 | all-reduce | flops 2 | bytes 16 | tf_op jit(solution)/shard_map/psum | solution.py:184
  890.5 73.4 %psum.104 = f32[2]{0:T(128)S(1)} all-reduce(f32[2]{0:T(128)S(1)} %get-tuple-element.15), channel_id=1, replica_groups=mesh['dom'=64,'kv'=4] {'dom','kv'}, use_global_device_ids=true, to_apply=%region_17.18 | all-reduce | flops 2 | bytes 16 | tf_op jit(solution)/shard_map/psum | solution.py:111
  964.1 13.6 fusion.60
  977.7 245.9 %all-reduce.11.cloned.1.call-done = f32[2,32768]{1,0:T(2,128)} async-done(((f32[2,32768]{1,0:T(2,128)}), f32[2,32768]{1,0:T(2,128)}) %all-reduce.11.cloned.1.call-update) | async-done | bytes 262160 | tf_op jit(solution)/shard_map/psum | solution.py:175
  1223.7 17.0 multiply_reduce_fusion.4
  1240.7 77.4 %psum.106 = f32[2]{0:T(128)S(1)} all-reduce(f32[2]{0:T(128)S(1)} %get-tuple-element.39), channel_id=1, replica_groups=mesh['dom'=64,'kv'=4] {'dom','kv'}, use_global_device_ids=true, to_apply=%region_20.21 | all-reduce | flops 2 | bytes 16 | tf_op jit(solution)/shard_map/psum | solution.py:184
  1318.3 73.5 %psum.107 = f32[2]{0:T(128)S(1)} all-reduce(f32[2]{0:T(128)S(1)} %get-tuple-element.13), channel_id=1, replica_groups=mesh['dom'=64,'kv'=4] {'dom','kv'}, use_global_device_ids=true, to_apply=%region_22.23 | all-reduce | flops 2 | bytes 16 | tf_op jit(solution)/shard_map/psum | solution.py:111
  1391.8 13.6 fusion.59
  1405.4 245.9 %all-reduce.13.cloned.1.call-done = f32[2,32768]{1,0:T(2,128)} async-done(((f32[2,32768]{1,0:T(2,128)}), f32[2,32768]{1,0:T(2,128)}) %all-reduce.13.cloned.1.call-update) | async-done | bytes 262160 | tf_op jit(solution)/shard_map/psum | solution.py:175
  1651.3 17.1 fusion.5
  1668.4 77.4 %psum.109 = f32[2]{0:T(128)S(1)} all-reduce(f32[2]{0:T(128)S(1)} %fusion.5), channel_id=1, replica_groups=mesh['dom'=64,'kv'=4] {'dom','kv'}, use_global_device_ids=true, to_apply=%region_25.26 | all-reduce | flops 2 | bytes 16 | tf_op jit(solution)/shard_map/psum | solution.py:184
  1746.0 7.8 psum.110
  1753.9 126.1 %psum.111 = f32[2]{0:T(128)S(1)} all-reduce(f32[2]{0:T(128)S(1)} %psum.110), channel_id=1, replica_groups=mesh['dom'=64,'kv'=4] {'dom'}, use_global_device_ids=true, to_apply=%region_28.29 | all-reduce | flops 2 | bytes 16 | tf_op jit(solution)/shard_map/psum | solution.py:192
  1879.9 0.6 fusion.66
  1881.9 0.5 subtract_bitcast_fusion
  (72 shorter events, 2.9 us)
Async XLA Ops:
  7.2 93.3 %copy-start = (bf16[384,128]{1,0:T(8,128)(2,1)S(1)}, bf16[384,128]{1,0:T(8,128)(2,1)}, u32[]{:S(2)}) copy-start(bf16[384,128]{1,0:T(8,128)(2,1)} %param.24) | copy-start | bytes 294916
  7.2 361.2 %all-reduce.7.cloned.1.call-start = ((), (), s32[]{:S(2)}) async-start(), calls=%async_computation | async-start | bytes 524288 | tf_op jit(solution)/shard_map/psum | solution.py:175
  10.0 72.5 %collective-permute-start.2 = (bf16[32,128]{1,0:T(8,128)(2,1)S(1)}, bf16[32,128]{1,0:T(8,128)(2,1)S(1)}, u32[]{:S(2)}, u32[]{:S(2)}) collective-permute-start(bf16[32,128]{1,0:T(8,128)(2,1)S(1)} %get-tuple-element.29), channel_id=1, source_target_pairs={{0,1},{1,2},{2,3},{3,4},{4,5},{5,6},{6,7},{7,8},{8,9},{9,10},{10,1... | collective-permute-start | bytes 24584 | tf_op jit(solution)/shard_map/ppermute | solution.py:20
  12.1 70.4 %collective-permute-start.3 = (bf16[32,128]{1,0:T(8,128)(2,1)S(1)}, bf16[32,128]{1,0:T(8,128)(2,1)S(1)}, u32[]{:S(2)}, u32[]{:S(2)}) collective-permute-start(bf16[32,128]{1,0:T(8,128)(2,1)S(1)} %get-tuple-element.30), channel_id=1, source_target_pairs={{1,0},{2,1},{3,2},{4,3},{5,4},{6,5},{7,6},{8,7},{9,8},{10,9},{11,1... | collective-permute-start | bytes 24584 | tf_op jit(solution)/shard_map/ppermute | solution.py:23
  15.5 43.0 %collective-permute-start = (f32[32,3]{1,0:T(8,128)S(1)}, f32[32,3]{1,0:T(8,128)S(1)}, u32[]{:S(2)}, u32[]{:S(2)}) collective-permute-start(f32[32,3]{1,0:T(8,128)S(1)} %get-tuple-element.27), channel_id=1, source_target_pairs={{0,1},{1,2},{2,3},{3,4},{4,5},{5,6},{6,7},{7,8},{8,9},{9,10},{10,1... | collective-permute-start | bytes 1160 | tf_op jit(solution)/shard_map/ppermute | solution.py:20
  15.6 42.9 %collective-permute-start.1 = (f32[32,3]{1,0:T(8,128)S(1)}, f32[32,3]{1,0:T(8,128)S(1)}, u32[]{:S(2)}, u32[]{:S(2)}) collective-permute-start(f32[32,3]{1,0:T(8,128)S(1)} %get-tuple-element.28), channel_id=1, source_target_pairs={{1,0},{2,1},{3,2},{4,3},{5,4},{6,5},{7,6},{8,7},{9,8},{10,9},{11,1... | collective-permute-start | bytes 1160 | tf_op jit(solution)/shard_map/ppermute | solution.py:23
  58.4 16.8 copy-start.3
  58.4 16.8 copy-start.4
  75.2 7.4 copy-start.2
  82.7 17.8 copy-start.1
  82.7 17.8 copy-start.5
  100.8 13.9 copy-start.6
  114.7 681.3 %all-reduce.9.cloned.1.call-start = ((), (), s32[]{:S(2)}) async-start(), calls=%async_computation.1 | async-start | bytes 524288 | tf_op jit(solution)/shard_map/psum | solution.py:175
  550.1 673.5 %all-reduce.11.cloned.1.call-start = ((), (), s32[]{:S(2)}) async-start(), calls=%async_computation.2 | async-start | bytes 524288 | tf_op jit(solution)/shard_map/psum | solution.py:175
  977.7 673.6 %all-reduce.13.cloned.1.call-start = ((), (), s32[]{:S(2)}) async-start(), calls=%async_computation.3 | async-start | bytes 524288 | tf_op jit(solution)/shard_map/psum | solution.py:175
Sparse Core Ops, SparseCore 0:
  114.9 253.4 all-reduce.6
  550.2 245.7 all-reduce.8
  977.8 245.8 all-reduce.10
  1405.6 245.7 all-reduce.12
